TPU v7x, 256 devices: a whole 4x4x8 slice. The times are simulated.
256 devices in a mesh: fsdp: 32 (over x_lo, z, core), ctx: 8 (over y, x_hi).
Axes of the slice: x: 4 (x_hi: 2, x_lo: 2; x = x_hi * 2 + x_lo), y: 4, z: 8, core: 2. Of those that a mesh axis runs over, the one named last changes fastest.
Arguments:
- tokens: bfloat16 [32, 4096, 4096], P('fsdp', 'ctx'), may hold values from -24 to 24
- w_query: bfloat16 [4096, 2, 128], P('fsdp'), may hold values from -0.09375 to 0.09375
- w_key: bfloat16 [4096, 2, 128], P('fsdp'), may hold values from -0.09375 to 0.09375
- w_value: bfloat16 [4096, 2, 4, 128], P('fsdp'), may hold values from -0.09375 to 0.09375
- w_out: bfloat16 [2, 4, 128, 4096], P(None, None, None, 'fsdp'), may hold values from -0.5 to 0.5
- value_experts: int32 [32, 4096, 2, 2], P('fsdp', 'ctx'), may hold values from 0 to 3, all different within a row
- value_gates: bfloat16 [32, 4096, 2, 2], P('fsdp', 'ctx'), may hold values from 0.25 to 1
- output_experts: int32 [32, 4096, 2, 2], P('fsdp', 'ctx'), may hold values from 0 to 3, all different within a row
- output_gates: bfloat16 [32, 4096, 2, 2], P('fsdp', 'ctx'), may hold values from 0.25 to 1
Outputs:
- projected: bfloat16 [32, 4096, 4096], P('fsdp', 'ctx')
Inputs may be any that keep to these rules, and one draw needn't show every extreme that they name: `value_experts`: each token and head names 2 different experts. `output_experts`: each token and head names 2 different experts.
All inputs are finite; a program needn't handle non-finite values.
Results may differ from a plain program's by a relative error of at most 0.015.
The roundings to bfloat16 on the way count: a program that leaves them out, or rounds other values in their place, can miss the bound.
Values may be sent and summed in bfloat16 or wider, within the bound.
No kernel may reach another device: no remote copies, remote signals or barrier semaphores. Data moves between devices by JAX's collectives and lax.ppermute only.
A program may use at most 128 MiB of HBM per device.

v0:
```python
import math

import jax
import jax.numpy as jnp
from jax import lax
from jax.sharding import PartitionSpec as P


def passed_along(shard, axis, by):
    count = lax.axis_size(axis)
    pairs = [(i, i + by) for i in range(count) if 0 <= i + by < count]
    return lax.ppermute(shard, axis, pairs)


def expert_mix(indices, gates, experts):
    one_hot = (indices[..., None] == jnp.arange(experts, dtype=jnp.int32)).astype(jnp.float32)
    return jnp.sum(gates.astype(jnp.float32)[..., None] * one_hot, axis=-2)


def attend(totals, queries, key_rows, value_rows, query_pos, key_start):
    run_max, run_sum, run_acc = totals
    scores = jnp.einsum(
        "qhd,khd->hqk", queries, key_rows, preferred_element_type=jnp.float32
    ) / math.sqrt(queries.shape[2])
    key_pos = key_start + jnp.arange(key_rows.shape[0], dtype=jnp.int32)
    visible = (query_pos[:, None] >= key_pos[None, :])[None]
    scores = jnp.where(visible, scores, -jnp.inf)
    new_max = jnp.maximum(run_max, jnp.max(scores, axis=-1))
    rescale = jnp.exp(run_max - new_max)
    weights = jnp.exp(scores - new_max[..., None])
    run_sum = run_sum * rescale + jnp.sum(weights, axis=-1)
    update = jnp.einsum(
        "hqk,khd->qhd", weights.astype(jnp.bfloat16), value_rows, preferred_element_type=jnp.float32
    )
    run_acc = run_acc * jnp.transpose(rescale)[:, :, None] + update
    return (new_max, run_sum, run_acc)


def on_device(
    tokens, w_query, w_key, w_value, w_out, value_experts, value_gates, output_experts, output_gates
):
    tok_rows = tokens.shape[1]
    inputs = tokens[0]
    head_count = w_query.shape[1]
    head_dim = w_query.shape[2]
    experts = w_value.shape[2]
    pieces = (
        lax.all_gather(w_query, "fsdp", axis=0, tiled=True),
        lax.all_gather(w_key, "fsdp", axis=0, tiled=True),
        lax.all_gather(w_value, "fsdp", axis=0, tiled=True),
    )
    piece_rows = pieces[0].shape[0]
    query_sum, key_sum, value_sum = tuple(
        (
            jnp.dot(inputs, panel.reshape(piece_rows, -1), preferred_element_type=jnp.float32)
            for panel in pieces
        )
    )
    queries = query_sum.astype(jnp.bfloat16).reshape(tok_rows, head_count, head_dim)
    key_rows = key_sum.astype(jnp.bfloat16).reshape(tok_rows, head_count, head_dim)
    value_mix = expert_mix(value_experts[0], value_gates[0], experts)
    value_rows = jnp.sum(
        value_mix[..., None] * value_sum.reshape(tok_rows, head_count, experts, head_dim), axis=2
    ).astype(jnp.bfloat16)
    cycle_size = lax.axis_size("ctx")
    cycle_pos = lax.axis_index("ctx")
    query_pos = cycle_pos * tok_rows + jnp.arange(tok_rows, dtype=jnp.int32)
    start_state = (
        jnp.full((head_count, tok_rows), -1e30, jnp.float32),
        jnp.zeros((head_count, tok_rows), jnp.float32),
        jnp.zeros((tok_rows, head_count, head_dim), jnp.float32),
    )
    kv_block = jnp.stack([key_rows, value_rows])
    first_state = attend(
        start_state, queries, key_rows, value_rows, query_pos, cycle_pos * tok_rows
    )

    def cycle_step(passes, bundle):
        totals, moving = bundle
        moving = passed_along(moving, "ctx", 1)
        owner = cycle_pos - passes - 1
        key_start = jnp.where(owner >= 0, owner * tok_rows, cycle_size * tok_rows)
        totals = attend(totals, queries, moving[0], moving[1], query_pos, key_start)
        return (totals, moving)

    final_state, unused_block = lax.fori_loop(
        0, cycle_size - 1, cycle_step, (first_state, kv_block)
    )
    run_max, run_sum, run_acc = final_state
    attended = (run_acc / jnp.transpose(run_sum)[:, :, None]).astype(jnp.bfloat16)
    output_mix = expert_mix(output_experts[0], output_gates[0], experts).astype(jnp.bfloat16)
    mixed_in = (
        output_mix.astype(jnp.float32)[..., None] * attended.astype(jnp.float32)[:, :, None, :]
    ).astype(jnp.bfloat16)
    mixed_flat = mixed_in.reshape(tok_rows, head_count * experts * head_dim)
    panel_piece = lax.all_gather(w_out, "fsdp", axis=3, tiled=True)
    result = jnp.dot(
        mixed_flat,
        panel_piece.reshape(-1, panel_piece.shape[3]),
        preferred_element_type=jnp.float32,
    )
    return result.astype(jnp.bfloat16)[None]


def solution(mesh):
    in_specs = (
        P("fsdp", "ctx", None),
        P("fsdp", None, None),
        P("fsdp", None, None),
        P("fsdp", None, None, None),
        P(None, None, None, "fsdp"),
        P("fsdp", "ctx", None, None),
        P("fsdp", "ctx", None, None),
        P("fsdp", "ctx", None, None),
        P("fsdp", "ctx", None, None),
    )
    out_specs = P("fsdp", "ctx", None)
    return jax.shard_map(
        on_device, mesh=mesh, in_specs=in_specs, out_specs=out_specs, check_vma=False
    )
```

profile of v0, /device:TPU:248, one launch (start us, length us, event | category | flops | bytes accessed | tf_op | source)
XLA Modules:
  0.0 401.1 jit_solution(15075435414131235273)
XLA Ops:
  6.5 0.7 all-gather.7.cloned.1.call-update
  7.3 0.7 all-gather.5.cloned.1.call-update
  8.1 0.7 all-gather.9.cloned.1.call-update
  8.8 0.5 all-gather.11.cloned.1.call-update
  9.3 0.7 bitcast_convert_fusion.2
  10.0 0.7 select_reduce_fusion.1
  10.8 0.7 bitcast_convert_fusion.1
  11.4 0.7 select_reduce_fusion
  12.2 0.2 broadcast_compare_fusion.1
  12.4 60.2 %all-gather.7.cloned.1.call-done = bf16[4096,2,128]{2,1,0:T(2,128)(2,1)} async-done(((bf16[128,2,128]{2,1,0:T(2,128)(2,1)}), bf16[4096,2,128]{2,1,0:T(2,128)(2,1)}) %all-gather.7.cloned.1.call-update) | async-done | bytes 2097168 | tf_op jit(solution)/shard_map/all_gather | solution.py:49
  72.6 4.2 %fusion.40 = bf16[512,256]{0,1:T(8,128)(2,1)S(1)} fusion(bf16[512,8,2,128]{3,2,1,0:T(2,128)(2,1)} %bitcast.103, bf16[1,512,4096]{2,1,0:T(8,128)(2,1)} %param.11), kind=kOutput, calls=%fused_computation.46 | convolution fusion | flops 1073872896 | bytes 6553600 | tf_op jit(solution)/shard_map/dot_general | solution.py:55
  76.9 61.9 %all-gather.5.cloned.1.call-done = bf16[4096,2,128]{2,1,0:T(2,128)(2,1)} async-done(((bf16[128,2,128]{2,1,0:T(2,128)(2,1)}), bf16[4096,2,128]{2,1,0:T(2,128)(2,1)}) %all-gather.5.cloned.1.call-update) | async-done | bytes 2097168 | tf_op jit(solution)/shard_map/all_gather | solution.py:48
  138.8 4.2 %fusion.35 = bf16[512,256]{0,1:T(8,128)(2,1)S(1)} fusion(bf16[512,8,2,128]{3,2,1,0:T(2,128)(2,1)} %bitcast.104, bf16[1,512,4096]{2,1,0:T(8,128)(2,1)} %param.11), kind=kOutput, calls=%fused_computation.45 | convolution fusion | flops 1073872896 | bytes 6553600 | tf_op jit(solution)/shard_map/dot_general | solution.py:55
  143.2 0.6 fusion.27
  143.8 0.5 fusion.33
  144.3 68.5 %all-gather.9.cloned.1.call-done = bf16[4096,2,4,128]{3,2,1,0:T(4,128)(2,1)} async-done(((bf16[128,2,4,128]{3,2,1,0:T(4,128)(2,1)}), bf16[4096,2,4,128]{3,2,1,0:T(4,128)(2,1)}) %all-gather.9.cloned.1.call-update) | async-done | bytes 8388624 | tf_op jit(solution)/shard_map/all_gather | solution.py:50
  212.8 13.8 %copy.52 = bf16[4096,2,4,128]{0,3,2,1:T(8,128)(2,1)} copy(bf16[4096,2,4,128]{3,2,1,0:T(4,128)(2,1)} %all-gather.9.cloned.1.call-done) | data formatting | bytes 16777216 | tf_op jit(solution)/shard_map/reshape | solution.py:55
  226.7 9.1 %multiply_reduce_fusion = bf16[512,2,128]{2,0,1:T(8,128)(2,1)} fusion(bf16[4096,2,4,128]{0,3,2,1:T(8,128)(2,1)} %copy.52, bf16[1,512,4096]{2,1,0:T(8,128)(2,1)} %param.11, f32[512,2,4]{0,2,1:T(4,128)S(1)} %select_reduce_fusion), kind=kOutput, calls=%fused_computation.37 | convolution fusion | flops 4295884800 | bytes 12861440 | tf_op jit(solution)/shard_map/dot_general | solution.py:55
  235.8 1.7 fusion.34
  237.7 1.0 pad_maximum_fusion
  238.7 147.3 %while.22 = (s32[]{:T(128)}, f32[2,512]{1,0:T(2,128)S(1)}, f32[2,512]{1,0:T(2,128)S(1)}, f32[512,2,128]{2,0,1:T(8,128)S(1)}, bf16[2,512,2,128]{3,1,2,0:T(8,128)(...) while((s32[]{:T(128)}, f32[2,512]{1,0:T(2,128)S(1)}, ...), condition=%wide.region_8.9_spmd.clone, body=%wide.region_5.8_spmd.clone.sunk | while | flops 274731008 | bytes 12394735 | solution.py:86
  238.7 4.9 %collective-permute-start = (bf16[2,512,2,128]{3,1,2,0:T(8,128)(2,1)S(1)}, bf16[2,512,2,128]{3,1,2,0:T(8,128)(2,1)S(1)}, u32[]{:S(2)}, u32[]{:S(2)}) collective-permute-start(bf16[2,512,2,128]{3,1,2,0:T(8,128)(2,1)S(1)} %get-tuple-element.353), channel_id=1, source_target_pairs={{0,1},{1,2},{2,3},{3,4},{4,5},{5,6},{6,7},{8,9},{9,10},{10,11},{11... | collective-permute-start | bytes 1572872 | tf_op jit(solution)/shard_map/while/body/eval_jaxpr/ppermute | solution.py:12
  243.6 0.2 broadcast_compare_fusion.3
  243.8 22.6 %collective-permute-done = bf16[2,512,2,128]{3,1,2,0:T(8,128)(2,1)S(1)} collective-permute-done((bf16[2,512,2,128]{3,1,2,0:T(8,128)(2,1)S(1)}, bf16[2,512,2,128]{3,1,2,0:T(8,128)(2,1)S(1)}, u32[]{:S(2)}, u32[]{:S(2)}) %collective-permute-start) | collective-permute-done | bytes 524320 | tf_op jit(solution)/shard_map/while/body/eval_jaxpr/ppermute | solution.py:12
  266.5 0.5 fusion.71
  267.0 0.5 fusion.73
  267.6 1.0 fusion.74
  268.6 2.6 collective-permute-start
  271.3 0.2 broadcast_compare_fusion.3
  271.5 25.0 %collective-permute-done = bf16[2,512,2,128]{3,1,2,0:T(8,128)(2,1)S(1)} collective-permute-done((bf16[2,512,2,128]{3,1,2,0:T(8,128)(2,1)S(1)}, bf16[2,512,2,128]{3,1,2,0:T(8,128)(2,1)S(1)}, u32[]{:S(2)}, u32[]{:S(2)}) %collective-permute-start) | collective-permute-done | bytes 524320 | tf_op jit(solution)/shard_map/while/body/eval_jaxpr/ppermute | solution.py:12
  296.5 0.5 fusion.71
  297.1 0.5 fusion.73
  297.7 1.0 fusion.74
  298.7 2.0 collective-permute-start
  300.7 0.2 broadcast_compare_fusion.3
  300.9 16.0 %collective-permute-done = bf16[2,512,2,128]{3,1,2,0:T(8,128)(2,1)S(1)} collective-permute-done((bf16[2,512,2,128]{3,1,2,0:T(8,128)(2,1)S(1)}, bf16[2,512,2,128]{3,1,2,0:T(8,128)(2,1)S(1)}, u32[]{:S(2)}, u32[]{:S(2)}) %collective-permute-start) | collective-permute-done | bytes 524320 | tf_op jit(solution)/shard_map/while/body/eval_jaxpr/ppermute | solution.py:12
  316.9 0.5 fusion.71
  317.4 0.5 fusion.73
  318.0 1.0 fusion.74
  319.0 3.4 collective-permute-start
  322.5 0.2 broadcast_compare_fusion.3
  322.7 12.2 %collective-permute-done = bf16[2,512,2,128]{3,1,2,0:T(8,128)(2,1)S(1)} collective-permute-done((bf16[2,512,2,128]{3,1,2,0:T(8,128)(2,1)S(1)}, bf16[2,512,2,128]{3,1,2,0:T(8,128)(2,1)S(1)}, u32[]{:S(2)}, u32[]{:S(2)}) %collective-permute-start) | collective-permute-done | bytes 524320 | tf_op jit(solution)/shard_map/while/body/eval_jaxpr/ppermute | solution.py:12
  334.9 0.5 fusion.71
  335.5 0.5 fusion.73
  336.1 1.0 fusion.74
  337.0 3.7 collective-permute-start
  340.8 0.2 broadcast_compare_fusion.3
  341.0 11.0 %collective-permute-done = bf16[2,512,2,128]{3,1,2,0:T(8,128)(2,1)S(1)} collective-permute-done((bf16[2,512,2,128]{3,1,2,0:T(8,128)(2,1)S(1)}, bf16[2,512,2,128]{3,1,2,0:T(8,128)(2,1)S(1)}, u32[]{:S(2)}, u32[]{:S(2)}) %collective-permute-start) | collective-permute-done | bytes 524320 | tf_op jit(solution)/shard_map/while/body/eval_jaxpr/ppermute | solution.py:12
  352.0 0.5 fusion.71
  352.6 0.5 fusion.73
  353.2 1.0 fusion.74
  354.2 4.0 collective-permute-start
  358.2 0.2 broadcast_compare_fusion.3
  358.4 9.9 %collective-permute-done = bf16[2,512,2,128]{3,1,2,0:T(8,128)(2,1)S(1)} collective-permute-done((bf16[2,512,2,128]{3,1,2,0:T(8,128)(2,1)S(1)}, bf16[2,512,2,128]{3,1,2,0:T(8,128)(2,1)S(1)}, u32[]{:S(2)}, u32[]{:S(2)}) %collective-permute-start) | collective-permute-done | bytes 524320 | tf_op jit(solution)/shard_map/while/body/eval_jaxpr/ppermute | solution.py:12
  368.2 0.5 fusion.71
  368.8 0.5 fusion.73
  369.4 1.0 fusion.74
  370.4 4.2 %collective-permute-start = (bf16[2,512,2,128]{3,1,2,0:T(8,128)(2,1)S(1)}, bf16[2,512,2,128]{3,1,2,0:T(8,128)(2,1)S(1)}, u32[]{:S(2)}, u32[]{:S(2)}) collective-permute-start(bf16[2,512,2,128]{3,1,2,0:T(8,128)(2,1)S(1)} %get-tuple-element.353), channel_id=1, source_target_pairs={{0,1},{1,2},{2,3},{3,4},{4,5},{5,6},{6,7},{8,9},{9,10},{10,11},{11... | collective-permute-start | bytes 1572872 | tf_op jit(solution)/shard_map/while/body/eval_jaxpr/ppermute | solution.py:12
  374.6 0.2 broadcast_compare_fusion.3
  374.8 9.0 %collective-permute-done = bf16[2,512,2,128]{3,1,2,0:T(8,128)(2,1)S(1)} collective-permute-done((bf16[2,512,2,128]{3,1,2,0:T(8,128)(2,1)S(1)}, bf16[2,512,2,128]{3,1,2,0:T(8,128)(2,1)S(1)}, u32[]{:S(2)}, u32[]{:S(2)}) %collective-permute-start) | collective-permute-done | bytes 524320 | tf_op jit(solution)/shard_map/while/body/eval_jaxpr/ppermute | solution.py:12
  383.8 0.5 fusion.71
  384.4 0.5 fusion.73
  385.0 1.0 fusion.74
  386.2 8.3 %fusion.17 = bf16[1,512,4096]{2,1,0:T(8,128)(2,1)} fusion(bf16[2,4,128,4096]{3,2,1,0:T(8,128)(2,1)} %all-gather.11.cloned.1.call-done, f32[512,2,128]{2,0,1:T(8,128)S(1)} %fusion.52, f32[512,2,4]{0,2,1:T(4,128)S(1)} %convert_element_type.118), kind=kOutput, calls=%fused_computation.26 | convolution fusion | flops 4298113024 | bytes 13123584 | tf_op jit(solution)/shard_map/dot_general | solution.py:97
  (48 shorter events, 1.4 us)
Async XLA Ops:
  6.5 66.0 %all-gather.7.cloned.1.call-start = ((), (), s32[]{:S(2)}) async-start(), calls=%async_computation.1 | async-start | bytes 2162688 | tf_op jit(solution)/shard_map/all_gather | solution.py:49
  7.3 131.6 %all-gather.5.cloned.1.call-start = ((), (), s32[]{:S(2)}) async-start(), calls=%async_computation | async-start | bytes 2162688 | tf_op jit(solution)/shard_map/all_gather | solution.py:48
  8.0 204.8 %all-gather.9.cloned.1.call-start = ((), (), s32[]{:S(2)}) async-start(), calls=%async_computation.2 | async-start | bytes 8650752 | tf_op jit(solution)/shard_map/all_gather | solution.py:50
  8.7 377.5 %all-gather.11.cloned.1.call-start = ((), (), s32[]{:S(2)}) async-start(), calls=%async_computation.3 | async-start | bytes 8650752 | tf_op jit(solution)/shard_map/all_gather | solution.py:96
  238.7 27.8 %collective-permute-start = (bf16[2,512,2,128]{3,1,2,0:T(8,128)(2,1)S(1)}, bf16[2,512,2,128]{3,1,2,0:T(8,128)(2,1)S(1)}, u32[]{:S(2)}, u32[]{:S(2)}) collective-permute-start(bf16[2,512,2,128]{3,1,2,0:T(8,128)(2,1)S(1)} %get-tuple-element.353), channel_id=1, source_target_pairs={{0,1},{1,2},{2,3},{3,4},{4,5},{5,6},{6,7},{8,9},{9,10},{10,11},{11... | collective-permute-start | bytes 1572872 | tf_op jit(solution)/shard_map/while/body/eval_jaxpr/ppermute | solution.py:12
  268.6 27.9 %collective-permute-start = (bf16[2,512,2,128]{3,1,2,0:T(8,128)(2,1)S(1)}, bf16[2,512,2,128]{3,1,2,0:T(8,128)(2,1)S(1)}, u32[]{:S(2)}, u32[]{:S(2)}) collective-permute-start(bf16[2,512,2,128]{3,1,2,0:T(8,128)(2,1)S(1)} %get-tuple-element.353), channel_id=1, source_target_pairs={{0,1},{1,2},{2,3},{3,4},{4,5},{5,6},{6,7},{8,9},{9,10},{10,11},{11... | collective-permute-start | bytes 1572872 | tf_op jit(solution)/shard_map/while/body/eval_jaxpr/ppermute | solution.py:12
  298.7 18.2 %collective-permute-start = (bf16[2,512,2,128]{3,1,2,0:T(8,128)(2,1)S(1)}, bf16[2,512,2,128]{3,1,2,0:T(8,128)(2,1)S(1)}, u32[]{:S(2)}, u32[]{:S(2)}) collective-permute-start(bf16[2,512,2,128]{3,1,2,0:T(8,128)(2,1)S(1)} %get-tuple-element.353), channel_id=1, source_target_pairs={{0,1},{1,2},{2,3},{3,4},{4,5},{5,6},{6,7},{8,9},{9,10},{10,11},{11... | collective-permute-start | bytes 1572872 | tf_op jit(solution)/shard_map/while/body/eval_jaxpr/ppermute | solution.py:12
  319.0 15.9 %collective-permute-start = (bf16[2,512,2,128]{3,1,2,0:T(8,128)(2,1)S(1)}, bf16[2,512,2,128]{3,1,2,0:T(8,128)(2,1)S(1)}, u32[]{:S(2)}, u32[]{:S(2)}) collective-permute-start(bf16[2,512,2,128]{3,1,2,0:T(8,128)(2,1)S(1)} %get-tuple-element.353), channel_id=1, source_target_pairs={{0,1},{1,2},{2,3},{3,4},{4,5},{5,6},{6,7},{8,9},{9,10},{10,11},{11... | collective-permute-start | bytes 1572872 | tf_op jit(solution)/shard_map/while/body/eval_jaxpr/ppermute | solution.py:12
  337.0 15.0 %collective-permute-start = (bf16[2,512,2,128]{3,1,2,0:T(8,128)(2,1)S(1)}, bf16[2,512,2,128]{3,1,2,0:T(8,128)(2,1)S(1)}, u32[]{:S(2)}, u32[]{:S(2)}) collective-permute-start(bf16[2,512,2,128]{3,1,2,0:T(8,128)(2,1)S(1)} %get-tuple-element.353), channel_id=1, source_target_pairs={{0,1},{1,2},{2,3},{3,4},{4,5},{5,6},{6,7},{8,9},{9,10},{10,11},{11... | collective-permute-start | bytes 1572872 | tf_op jit(solution)/shard_map/while/body/eval_jaxpr/ppermute | solution.py:12
  354.2 14.1 %collective-permute-start = (bf16[2,512,2,128]{3,1,2,0:T(8,128)(2,1)S(1)}, bf16[2,512,2,128]{3,1,2,0:T(8,128)(2,1)S(1)}, u32[]{:S(2)}, u32[]{:S(2)}) collective-permute-start(bf16[2,512,2,128]{3,1,2,0:T(8,128)(2,1)S(1)} %get-tuple-element.353), channel_id=1, source_target_pairs={{0,1},{1,2},{2,3},{3,4},{4,5},{5,6},{6,7},{8,9},{9,10},{10,11},{11... | collective-permute-start | bytes 1572872 | tf_op jit(solution)/shard_map/while/body/eval_jaxpr/ppermute | solution.py:12
  370.4 13.5 %collective-permute-start = (bf16[2,512,2,128]{3,1,2,0:T(8,128)(2,1)S(1)}, bf16[2,512,2,128]{3,1,2,0:T(8,128)(2,1)S(1)}, u32[]{:S(2)}, u32[]{:S(2)}) collective-permute-start(bf16[2,512,2,128]{3,1,2,0:T(8,128)(2,1)S(1)} %get-tuple-element.353), channel_id=1, source_target_pairs={{0,1},{1,2},{2,3},{3,4},{4,5},{5,6},{6,7},{8,9},{9,10},{10,11},{11... | collective-permute-start | bytes 1572872 | tf_op jit(solution)/shard_map/while/body/eval_jaxpr/ppermute | solution.py:12
Sparse Core Ops, SparseCore 0:
  9.2 63.2 all-gather.6
  74.4 64.3 all-gather.4
  140.7 72.0 all-gather.8
  214.4 96.4 all-gather.10
where the time goes:
time: 402 us; the launch traced here: 401 us
  waiting for transfers between devices  299 us (74%)
  matrix products  38.6 us (10%)
  starting transfers between devices  25 us (6%)
  local copies, waits for them, and re-layouts  14.6 us (4%)
  between operations  13.2 us (3%)
  other arithmetic  9.98 us (2%)
    ppermute x7, waiting for transfers between devices, passed_along(): return lax.ppermute(shard, axis, pairs)  106 us
    all_gather x1, waiting for transfers between devices, on_device(): lax.all_gather(w_value, 'fsdp', axis=0, tiled=True)  68.5 us
    all_gather x1, waiting for transfers between devices, on_device(): lax.all_gather(w_query, 'fsdp', axis=0, tiled=True)  61.9 us
    all_gather x1, waiting for transfers between devices, on_device(): lax.all_gather(w_key, 'fsdp', axis=0, tiled=True)  60.2 us
    ppermute x7, starting transfers between devices, passed_along(): return lax.ppermute(shard, axis, pairs)  24.9 us
    dot_general x3, matrix products, on_device(): jnp.dot(inputs, panel.reshape(piece_rows, -1), preferred_element_type=jnp...  17.4 us
    reshape x1, local copies, waits for them, and re-layouts, on_device(): panel.reshape(piece_rows, -1)  13.8 us
    dot_general x8, matrix products, attend(): jnp.einsum('hqk,khd->qhd', weights.astype(jnp.bfloat16), value_rows, pref...  8.41 us
  transfers between devices with their start and end apart: 11, of which 10 were waited for; matrix products, arithmetic and copies ran while one was open for 14% of the time, Pallas kernels for 0%

commit v1 on v0

v1 whole, which is shorter than its diff:
```python
import functools
import math

import jax
import jax.numpy as jnp
from jax import lax
from jax.experimental import pallas as pl
from jax.experimental.pallas import tpu as pltpu
from jax.sharding import Mesh
from jax.sharding import PartitionSpec as P

AXES = ("x_lo", "z", "core", "y", "x_hi")
SIZES = (2, 8, 2, 4, 2)
FSDP = ("x_lo", "z", "core")
CTX = ("y", "x_hi")
HEADS, EXPERTS, DH = 2, 4, 128
WIDTH = HEADS * DH
MIB = 1 << 20


def expert_mix(indices, gates):
    one_hot = (indices[..., None] == jnp.arange(EXPERTS, dtype=jnp.int32)).astype(jnp.float32)
    mix = jnp.sum(gates.astype(jnp.float32)[..., None] * one_hot, axis=-2)
    return mix.reshape(mix.shape[0], HEADS * EXPERTS)


def project_kernel(x_ref, w_ref, mix_ref, q_ref, kv_ref, acc_ref):
    n = pl.program_id(0)
    block = jnp.dot(x_ref[...], w_ref[...], preferred_element_type=jnp.float32)

    @pl.when(n == 0)
    def _():
        q_ref[...] = block.astype(jnp.bfloat16)

    @pl.when(n == 1)
    def _():
        kv_ref[:, :WIDTH] = block.astype(jnp.bfloat16)

    for head in range(HEADS):
        for half in range(2):

            @pl.when(n == 2 + 2 * head + half)
            def _():
                first = head * EXPERTS + 2 * half
                part = (
                    mix_ref[:, first : first + 1] * block[:, :DH]
                    + mix_ref[:, first + 1 : first + 2] * block[:, DH:]
                )
                if half == 0:
                    acc_ref[...] = part
                else:
                    start = WIDTH + head * DH
                    kv_ref[:, start : start + DH] = (acc_ref[...] + part).astype(jnp.bfloat16)


def project(x, w, mix):
    rows, depth = x.shape
    columns = w.shape[1]
    return pl.pallas_call(
        project_kernel,
        grid=(columns // WIDTH,),
        in_specs=[
            pl.BlockSpec((rows, depth), lambda n: (0, 0)),
            pl.BlockSpec((depth, WIDTH), lambda n: (0, n)),
            pl.BlockSpec((rows, HEADS * EXPERTS), lambda n: (0, 0)),
        ],
        out_specs=[
            pl.BlockSpec((rows, WIDTH), lambda n: (0, 0)),
            pl.BlockSpec((rows, 2 * WIDTH), lambda n: (0, 0)),
        ],
        out_shape=[
            jax.ShapeDtypeStruct((rows, WIDTH), jnp.bfloat16),
            jax.ShapeDtypeStruct((rows, 2 * WIDTH), jnp.bfloat16),
        ],
        scratch_shapes=[pltpu.VMEM((rows, DH), jnp.float32)],
        compiler_params=pltpu.CompilerParams(vmem_limit_bytes=40 * MIB),
        cost_estimate=pl.CostEstimate(
            flops=2 * rows * depth * columns,
            bytes_accessed=2 * (rows * depth + depth * columns),
            transcendentals=0,
        ),
    )(x, w, mix)


def attend_kernel(count, place_ref, q_ref, mix_ref, *refs):
    kv_refs, out_ref = refs[:count], refs[count]
    m_ref, l_ref, acc_ref = refs[count + 1 :]
    place = place_ref[0]
    rows = q_ref.shape[0]
    scale = 1.0 / math.sqrt(DH)
    for head in range(HEADS):
        lanes = slice(head * DH, (head + 1) * DH)

        def step(k, lanes=lanes, head=head):
            kv = kv_refs[k]
            scores = (
                lax.dot_general(
                    q_ref[:, lanes],
                    kv[:, lanes],
                    (((1,), (1,)), ((), ())),
                    preferred_element_type=jnp.float32,
                )
                * scale
            )
            values = kv[:, WIDTH + head * DH : WIDTH + (head + 1) * DH]
            if k == 0:
                q_pos = lax.broadcasted_iota(jnp.int32, scores.shape, 0)
                k_pos = lax.broadcasted_iota(jnp.int32, scores.shape, 1)
                scores = jnp.where(q_pos >= k_pos, scores, -jnp.inf)
                top = jnp.max(scores, axis=1, keepdims=True)
                weights = jnp.exp(scores - top)
                m_ref[head] = top
                l_ref[head] = jnp.sum(weights, axis=1, keepdims=True)
                acc_ref[:, lanes] = jnp.dot(
                    weights.astype(jnp.bfloat16), values, preferred_element_type=jnp.float32
                )
            else:
                before = m_ref[head]
                top = jnp.maximum(before, jnp.max(scores, axis=1, keepdims=True))
                rescale = jnp.exp(before - top)
                weights = jnp.exp(scores - top)
                m_ref[head] = top
                l_ref[head] = l_ref[head] * rescale + jnp.sum(weights, axis=1, keepdims=True)
                acc_ref[:, lanes] = acc_ref[:, lanes] * rescale + jnp.dot(
                    weights.astype(jnp.bfloat16), values, preferred_element_type=jnp.float32
                )

        for k in range(count):
            if k == 0:
                step(0)
            else:
                pl.when(place >= k)(functools.partial(step, k))
        attended = (acc_ref[:, lanes] / l_ref[head]).astype(jnp.bfloat16).astype(jnp.float32)
        for expert in range(EXPERTS):
            index = head * EXPERTS + expert
            out_ref[:, index * DH : (index + 1) * DH] = (
                mix_ref[:, index : index + 1] * attended
            ).astype(jnp.bfloat16)


def attend(place, q, mix, blocks):
    rows = q.shape[0]
    count = len(blocks)
    return pl.pallas_call(
        functools.partial(attend_kernel, count),
        in_specs=[pl.BlockSpec(memory_space=pltpu.SMEM)]
        + [pl.BlockSpec(memory_space=pltpu.VMEM)] * (2 + count),
        out_specs=pl.BlockSpec(memory_space=pltpu.VMEM),
        out_shape=jax.ShapeDtypeStruct((rows, HEADS * EXPERTS * DH), jnp.bfloat16),
        scratch_shapes=[
            pltpu.VMEM((HEADS, rows, 1), jnp.float32),
            pltpu.VMEM((HEADS, rows, 1), jnp.float32),
            pltpu.VMEM((rows, WIDTH), jnp.float32),
        ],
        compiler_params=pltpu.CompilerParams(vmem_limit_bytes=40 * MIB),
        cost_estimate=pl.CostEstimate(
            flops=4 * rows * rows * DH * HEADS * count,
            bytes_accessed=2 * rows * WIDTH * 2 * count,
            transcendentals=rows * rows * HEADS * count,
        ),
    )(place, q, mix, *blocks)


PANELS = 4


def output_kernel(a_ref, w_ref, o_ref):
    panel = jnp.concatenate([w_ref[i] for i in range(PANELS)], axis=1)
    o_ref[...] = jnp.dot(a_ref[...], panel, preferred_element_type=jnp.float32).astype(jnp.bfloat16)


def output(mixed, panels):
    rows, depth = mixed.shape
    count, _, width = panels.shape
    return pl.pallas_call(
        output_kernel,
        grid=(count // PANELS,),
        in_specs=[
            pl.BlockSpec((rows, depth), lambda n: (0, 0)),
            pl.BlockSpec((PANELS, depth, width), lambda n: (n, 0, 0)),
        ],
        out_specs=pl.BlockSpec((rows, PANELS * width), lambda n: (0, n)),
        out_shape=jax.ShapeDtypeStruct((rows, count * width), jnp.bfloat16),
        compiler_params=pltpu.CompilerParams(vmem_limit_bytes=40 * MIB),
        cost_estimate=pl.CostEstimate(
            flops=2 * rows * depth * count * width,
            bytes_accessed=2 * (rows * count * width + depth * count * width),
            transcendentals=0,
        ),
    )(mixed, panels)


def on_device(
    tokens, w_query, w_key, w_value, w_out, value_experts, value_gates, output_experts, output_gates
):
    x = tokens[0]
    shard = w_query.shape[0]
    w_all = jnp.concatenate(
        [w.reshape(shard, -1) for w in (w_query, w_key, w_value)], axis=1
    )
    w_all = lax.all_gather(w_all, FSDP, axis=0, tiled=True)
    panel = w_out.reshape(-1, w_out.shape[3])
    panels = lax.all_gather(panel, FSDP, axis=0, tiled=False)
    value_mix = expert_mix(value_experts[0], value_gates[0])
    output_mix = expert_mix(output_experts[0], output_gates[0])
    output_mix = output_mix.astype(jnp.bfloat16).astype(jnp.float32)
    q, kv = project(x, w_all, value_mix)
    count = lax.axis_size(CTX)
    place = lax.axis_index(CTX)
    blocks = [kv] + [
        lax.ppermute(kv, CTX, [(i, i + k) for i in range(count - k)]) for k in range(1, count)
    ]
    mixed = attend(place.astype(jnp.int32).reshape(1), q, output_mix, blocks)
    return output(mixed, panels)[None]


def solution(mesh):
    grid = Mesh(mesh.devices.reshape(SIZES), AXES)
    seq = P(FSDP, CTX, None, None)
    in_specs = (
        P(FSDP, CTX, None),
        P(FSDP, None, None),
        P(FSDP, None, None),
        P(FSDP, None, None, None),
        P(None, None, None, FSDP),
        seq,
        seq,
        seq,
        seq,
    )
    return jax.shard_map(
        on_device, mesh=grid, in_specs=in_specs, out_specs=P(FSDP, CTX, None), check_vma=False
    )
```

time: 402 us -> 238 us (0.59)
  the two profiles are of different devices: /device:TPU:248 before, /device:TPU:31 now
where the time goes in v1:
time: 238 us; the launch traced here: 237 us
  waiting for transfers between devices  162 us (68%)
  Pallas kernels  38.6 us (16%)
  between operations  13.6 us (6%)
  local copies, waits for them, and re-layouts  11.7 us (5%)
  starting transfers between devices  9.07 us (4%)
    all_gather x1, waiting for transfers between devices, on_device(): w_all = lax.all_gather(w_all, FSDP, axis=0, tiled=True)  80.7 us
    ppermute x7, waiting for transfers between devices, on_device(): lax.ppermute(kv, CTX, [(i, i + k) for i in range(count - k)])  80.6 us
    pallas_call x1, Pallas kernels, attend(): pl.pallas_call(functools.partial(attend_kernel, count), in_specs=[pl.Bloc...  21.3 us
    pallas_call x1, Pallas kernels, project(): pl.pallas_call(project_kernel, grid=(columns // WIDTH,), in_specs=[pl.Blo...  10.6 us
    unnamed x16, local copies, waits for them, and re-layouts  9.41 us
    ppermute x7, starting transfers between devices, on_device(): lax.ppermute(kv, CTX, [(i, i + k) for i in range(count - k)])  9.02 us
    pallas_call x1, Pallas kernels, output(): pl.pallas_call(output_kernel, grid=(count // PANELS,), in_specs=[pl.Block...  6.75 us
  transfers between devices with their start and end apart: 9, of which 5 were waited for; matrix products, arithmetic and copies ran while one was open for 1% of the time, Pallas kernels for 13%

profile of v1, /device:TPU:31, one launch (start us, length us, event | category | flops | bytes accessed | tf_op | source)
XLA Modules:
  0.0 237.2 jit_solution(4144219823084609167)
XLA Ops:
  6.5 0.0 all-gather.3.cloned.1.call-start
  6.5 1.1 reshape.38
  7.7 0.9 copy_bitcast_fusion
  8.5 0.8 pad_maximum_fusion
  9.3 0.0 all-gather.3.cloned.1.call-update
  9.3 0.0 all-gather.5.cloned.1.call-start
  9.4 0.7 all-gather.5.cloned.1.call-update
  10.1 0.7 bitcast_convert_fusion.1
  10.8 0.7 select_reduce_fusion.1
  11.5 0.1 copy.26.mix_ref
  11.7 80.7 %all-gather.3.cloned.1.call-done.w_ref = bf16[4096,1536]{1,0:T(8,128)(2,1)} async-done(((bf16[128,1536]{1,0:T(8,128)(2,1)}), bf16[4096,1536]{1,0:T(8,128)(2,1)}) %all-gather.3.cloned.1.call-update) | async-done | bytes 12582928 | tf_op jit(solution)/shard_map/all_gather | solution.py:201
  92.3 0.0 copy-start.1
  92.3 2.2 copy-done.1
  94.5 0.0 copy-start.7
  94.5 0.0 copy-start.6
  94.5 10.6 %shard_map.91 = (bf16[512,256]{1,0:T(8,128)(2,1)S(1)}, bf16[512,512]{1,0:T(8,128)(2,1)S(1)}) custom-call(bf16[512,4096]{1,0:T(8,128)(2,1)S(1)} %bitcast.22, bf16[4096,1536]{1,0:T(8,128)(2,1)} %all-gather.3.cloned.1.call-done.w_ref, f32[512,8]{1,0:T(8,128)S(1)} %copy.26.mix_ref), custom_call_target="tpu_custom_call" | custom-call | flops 6442450944 | bytes 16777216 | tf_op jit(solution)/shard_map/pallas_call | solution.py:59
  105.1 0.0 copy-start.4
  105.1 0.7 copy-done.4
  105.8 1.3 collective-permute-start
  107.1 1.3 collective-permute-start.1
  108.4 1.3 collective-permute-start.2
  109.7 1.3 collective-permute-start.3
  111.0 1.3 collective-permute-start.4
  112.3 21.8 %collective-permute-done.refs_1_ = bf16[512,512]{1,0:T(8,128)(2,1)S(1)} collective-permute-done((bf16[512,512]{1,0:T(8,128)(2,1)S(1)}, bf16[512,512]{1,0:T(8,128)(2,1)S(1)}, u32[]{:S(2)}, u32[]{:S(2)}) %collective-permute-start) | collective-permute-done | bytes 524320 | tf_op jit(solution)/shard_map/ppermute | solution.py:211
  134.1 1.3 collective-permute-start.5
  135.4 0.0 collective-permute-done.1.refs_2_
  135.4 1.3 collective-permute-start.6
  136.7 0.0 copy-done.7
  136.8 0.0 copy-done.6
  136.8 0.1 copy.27.mix_ref
  136.9 19.9 %collective-permute-done.2.refs_3_ = bf16[512,512]{1,0:T(8,128)(2,1)S(1)} collective-permute-done((bf16[512,512]{1,0:T(8,128)(2,1)S(1)}, bf16[512,512]{1,0:T(8,128)(2,1)S(1)}, u32[]{:S(2)}, u32[]{:S(2)}) %collective-permute-start.2) | collective-permute-done | bytes 524320 | tf_op jit(solution)/shard_map/ppermute | solution.py:211
  156.9 0.0 collective-permute-done.3.refs_4_
  156.9 23.1 %collective-permute-done.4.refs_5_ = bf16[512,512]{1,0:T(8,128)(2,1)S(1)} collective-permute-done((bf16[512,512]{1,0:T(8,128)(2,1)S(1)}, bf16[512,512]{1,0:T(8,128)(2,1)S(1)}, u32[]{:S(2)}, u32[]{:S(2)}) %collective-permute-start.4) | collective-permute-done | bytes 524320 | tf_op jit(solution)/shard_map/ppermute | solution.py:211
  179.9 0.0 collective-permute-done.5.refs_6_
  179.9 15.8 %collective-permute-done.6.refs_7_ = bf16[512,512]{1,0:T(8,128)(2,1)} collective-permute-done((bf16[512,512]{1,0:T(8,128)(2,1)S(1)}, bf16[512,512]{1,0:T(8,128)(2,1)}, u32[]{:S(2)}, u32[]{:S(2)}) %collective-permute-start.6) | collective-permute-done | bytes 524320 | tf_op jit(solution)/shard_map/ppermute | solution.py:211
  195.8 0.0 copy-start.5
  195.8 0.9 copy-done.5
  196.7 21.3 %shard_map.92.a_ref = bf16[512,1024]{1,0:T(8,128)(2,1)S(1)} custom-call(s32[1]{0:T(128)} %bitcast.place_ref, bf16[512,256]{1,0:T(8,128)(2,1)S(1)} %copy-done.5, f32[512,8]{1,0:T(8,128)S(1)} %copy.27.mix_ref, bf16[512,512]{1,0:T(8,128)(2,1)S(1)} %get-tuple-element.8.refs_0_, bf16[512,512]{1,0:T(8,128)(2,1)S(1)} %collective-permute-done.refs_1_, ...), custom_call_target="tpu_custom_call" | custom-call | flops 2147483648 | bytes 4194304 | tf_op jit(solution)/shard_map/pallas_call | solution.py:144
  218.0 0.0 copy-start.2
  218.1 1.0 copy-done.2
  219.0 0.0 all-gather.5.cloned.1.call-done.w_ref
  219.0 0.0 copy-start
  219.0 3.4 %copy-done = bf16[32,1024,128]{2,1,0:T(8,128)(2,1)S(1)} copy-done((bf16[32,1024,128]{2,1,0:T(8,128)(2,1)S(1)}, bf16[32,1024,128]{2,1,0:T(8,128)(2,1)}, u32[]{:S(2)}) %copy-start) | copy-done | bytes 8388632
  222.4 0.0 copy-start.3
  222.4 1.2 copy-done.3
  223.6 6.7 %shard_map.93 = bf16[512,4096]{1,0:T(8,128)(2,1)} custom-call(bf16[512,1024]{1,0:T(8,128)(2,1)S(1)} %copy-done.3, bf16[32,1024,128]{2,1,0:T(8,128)(2,1)S(1)} %copy-done), custom_call_target="tpu_custom_call" | custom-call | flops 4294967296 | bytes 12582912 | tf_op jit(solution)/shard_map/pallas_call | solution.py:175
  (4 shorter events, 0.0 us)
Async XLA Ops:
  6.5 85.8 %all-gather.3.cloned.1.call-start = ((), (), s32[]{:S(2)}) async-start(), calls=%async_computation | async-start | bytes 12976128 | tf_op jit(solution)/shard_map/all_gather | solution.py:201
  9.3 209.7 %all-gather.5.cloned.1.call-start = ((), (), s32[]{:S(2)}) async-start(), calls=%async_computation.1 | async-start | bytes 8650752 | tf_op jit(solution)/shard_map/all_gather | solution.py:203
  92.3 2.2 copy-start.1
  94.5 42.2 %copy-start.7 = (bf16[1,512,2,2]{1,3,2,0:T(2,128)(2,1)S(1)}, bf16[1,512,2,2]{1,3,2,0:T(2,128)(2,1)}, u32[]{:S(2)}) copy-start(bf16[1,512,2,2]{1,3,2,0:T(2,128)(2,1)} %param.17) | copy-start | bytes 12292
  94.5 42.2 %copy-start.6 = (s32[1,512,2,2]{1,3,2,0:T(2,128)S(1)}, s32[1,512,2,2]{1,3,2,0:T(2,128)}, u32[]{:S(2)}) copy-start(s32[1,512,2,2]{1,3,2,0:T(2,128)} %param.16) | copy-start | bytes 24580
  105.1 0.7 copy-start.4
  105.8 28.3 %collective-permute-start = (bf16[512,512]{1,0:T(8,128)(2,1)S(1)}, bf16[512,512]{1,0:T(8,128)(2,1)S(1)}, u32[]{:S(2)}, u32[]{:S(2)}) collective-permute-start(bf16[512,512]{1,0:T(8,128)(2,1)S(1)} %get-tuple-element.8.refs_0_), channel_id=1, source_target_pairs={{0,1},{1,2},{2,3},{3,4},{4,5},{5,6},{6,7},{8,9},{9,10},{10,11},{11... | collective-permute-start | bytes 1572872 | tf_op jit(solution)/shard_map/ppermute | solution.py:211
  107.1 28.3 %collective-permute-start.1 = (bf16[512,512]{1,0:T(8,128)(2,1)S(1)}, bf16[512,512]{1,0:T(8,128)(2,1)S(1)}, u32[]{:S(2)}, u32[]{:S(2)}) collective-permute-start(bf16[512,512]{1,0:T(8,128)(2,1)S(1)} %get-tuple-element.8.refs_0_), channel_id=1, source_target_pairs={{0,2},{1,3},{2,4},{3,5},{4,6},{5,7},{8,10},{9,11},{10,12},{11,13},... | collective-permute-start | bytes 1572872 | tf_op jit(solution)/shard_map/ppermute | solution.py:211
  108.4 48.5 %collective-permute-start.2 = (bf16[512,512]{1,0:T(8,128)(2,1)S(1)}, bf16[512,512]{1,0:T(8,128)(2,1)S(1)}, u32[]{:S(2)}, u32[]{:S(2)}) collective-permute-start(bf16[512,512]{1,0:T(8,128)(2,1)S(1)} %get-tuple-element.8.refs_0_), channel_id=1, source_target_pairs={{0,3},{1,4},{2,5},{3,6},{4,7},{8,11},{9,12},{10,13},{11,14},{12,15... | collective-permute-start | bytes 1572872 | tf_op jit(solution)/shard_map/ppermute | solution.py:211
  109.7 47.2 %collective-permute-start.3 = (bf16[512,512]{1,0:T(8,128)(2,1)S(1)}, bf16[512,512]{1,0:T(8,128)(2,1)S(1)}, u32[]{:S(2)}, u32[]{:S(2)}) collective-permute-start(bf16[512,512]{1,0:T(8,128)(2,1)S(1)} %get-tuple-element.8.refs_0_), channel_id=1, source_target_pairs={{0,4},{1,5},{2,6},{3,7},{8,12},{9,13},{10,14},{11,15},{16,20},{17,... | collective-permute-start | bytes 1572872 | tf_op jit(solution)/shard_map/ppermute | solution.py:211
  111.0 68.9 %collective-permute-start.4 = (bf16[512,512]{1,0:T(8,128)(2,1)S(1)}, bf16[512,512]{1,0:T(8,128)(2,1)S(1)}, u32[]{:S(2)}, u32[]{:S(2)}) collective-permute-start(bf16[512,512]{1,0:T(8,128)(2,1)S(1)} %get-tuple-element.8.refs_0_), channel_id=1, source_target_pairs={{0,5},{1,6},{2,7},{8,13},{9,14},{10,15},{16,21},{17,22},{18,23},{2... | collective-permute-start | bytes 1572872 | tf_op jit(solution)/shard_map/ppermute | solution.py:211
  134.1 45.8 %collective-permute-start.5 = (bf16[512,512]{1,0:T(8,128)(2,1)S(1)}, bf16[512,512]{1,0:T(8,128)(2,1)}, u32[]{:S(2)}, u32[]{:S(2)}) collective-permute-start(bf16[512,512]{1,0:T(8,128)(2,1)S(1)} %get-tuple-element.8.refs_0_), channel_id=1, source_target_pairs={{0,6},{1,7},{8,14},{9,15},{16,22},{17,23},{24,30},{25,31},{32,38},... | collective-permute-start | bytes 1572872 | tf_op jit(solution)/shard_map/ppermute | solution.py:211
  135.4 60.3 %collective-permute-start.6 = (bf16[512,512]{1,0:T(8,128)(2,1)S(1)}, bf16[512,512]{1,0:T(8,128)(2,1)}, u32[]{:S(2)}, u32[]{:S(2)}) collective-permute-start(bf16[512,512]{1,0:T(8,128)(2,1)S(1)} %get-tuple-element.8.refs_0_), channel_id=1, source_target_pairs={{0,7},{8,15},{16,23},{24,31},{32,39},{40,47},{48,55},{56,63},{64,7... | collective-permute-start | bytes 1572872 | tf_op jit(solution)/shard_map/ppermute | solution.py:211
  195.8 1.0 copy-start.5
  218.0 1.0 copy-start.2
  219.0 3.4 %copy-start = (bf16[32,1024,128]{2,1,0:T(8,128)(2,1)S(1)}, bf16[32,1024,128]{2,1,0:T(8,128)(2,1)}, u32[]{:S(2)}) copy-start(bf16[32,1024,128]{2,1,0:T(8,128)(2,1)} %all-gather.5.cloned.1.call-done.w_ref) | copy-start | bytes 25165828
  222.4 1.2 copy-start.3
Sparse Core Ops, SparseCore 0:
  9.5 82.8 all-gather.2
  94.2 72.2 all-gather.4
